TPU v7x, 256 devices: a whole 4x4x8 slice. The times are simulated.
256 devices in a mesh: row: 8 (over z), col: 16 (over x, y_lo, core), rep: 2 (over y_hi).
Axes of the slice: x: 4, y: 4 (y_hi: 2, y_lo: 2; y = y_hi * 2 + y_lo), z: 8, core: 2. Of those that a mesh axis runs over, the one named last changes fastest.
Arguments:
- a_blocks: bfloat16 [16384, 4096], P('row', 'col'), may hold values from -6 to 6
- a_mask: int32 [64, 16], P('row', 'col'), may hold values from 0 to 1, as said below
- b_blocks: bfloat16 [4096, 8192], P('row', 'col'), may hold values from -0.09375 to 0.09375
- b_mask: int32 [16, 32], P('row', 'col'), may hold values from 0 to 1
Outputs:
- c_product: bfloat16 [16384, 8192], P('row', ('col', 'rep'))
Inputs may be any that keep to these rules, and one draw needn't show every extreme that they name: a_mask holds 0 or 1; within each aligned tile of 8 block rows by 1 inner blocks (one device's tile) at most 2 entries are 1, and some tile holds exactly 2.
All inputs are finite; a program needn't handle non-finite values.
Results may differ from a plain program's by a relative error of at most 0.007.
Values may be sent and summed in bfloat16 or wider, within the bound.
A program may use at most 64 MiB of HBM per device.

v0:
```python
import jax
import jax.numpy as jnp
from jax import lax
from jax.sharding import PartitionSpec as P

BS = 256


def from_everyone(shard, axis):
    length = lax.axis_size(axis)
    return lax.all_to_all(
        jnp.broadcast_to(shard[None], (length, *shard.shape)), axis, 0, 0, tiled=True
    )


def in_order(pieces, dim):
    pieces = jnp.moveaxis(pieces, 0, dim)
    shape = pieces.shape
    return pieces.reshape(*shape[:dim], shape[dim] * shape[dim + 1], *shape[dim + 2 :])


def gather_directly(shard, axis, dim):
    pieces = from_everyone(shard, axis)
    return in_order(pieces, dim)


def expand(values, pattern):
    block_rows = pattern.shape[0]
    block_cols = pattern.shape[1]
    shaped = values.reshape(block_rows, BS, block_cols, BS) * pattern[:, None, :, None].astype(
        jnp.bfloat16
    )
    return shaped.reshape(block_rows * BS, block_cols * BS)


def pack_blocks(a_blocks, a_mask):
    block_rows = a_mask.shape[0]
    block_cols = a_mask.shape[1]
    slot_count = max(block_rows // 4, 1)
    flat_mask = a_mask.reshape(-1)
    slot_of = jnp.cumsum(flat_mask) - 1
    slot_ids = jnp.arange(slot_count, dtype=jnp.int32)[:, None]
    chosen = (flat_mask[None, :] == 1) & (slot_of[None, :] == slot_ids)
    flat_blocks = (
        a_blocks.reshape(block_rows, BS, block_cols, BS)
        .transpose(0, 2, 1, 3)
        .reshape(block_rows * block_cols, BS * BS)
    )
    packed = jnp.dot(
        chosen.astype(jnp.bfloat16), flat_blocks, preferred_element_type=jnp.float32
    ).astype(jnp.bfloat16)
    positions = jnp.arange(block_rows * block_cols, dtype=jnp.int32)
    chosen_int = chosen.astype(jnp.int32)
    used = jnp.sum(chosen_int, axis=1) > 0
    block_row = jnp.where(
        used, jnp.sum(chosen_int * (positions // block_cols)[None, :], axis=1), block_rows
    )
    block_inner = jnp.where(
        used, jnp.sum(chosen_int * (positions % block_cols)[None, :], axis=1), 0
    )
    codes = jnp.stack([block_row, block_inner], axis=1)
    return (packed.reshape(slot_count, BS, BS), codes)


def per_device(a_blocks, a_mask, b_blocks, b_mask):
    masked_b = expand(b_blocks, b_mask)
    layer_index = lax.axis_index("rep")
    c_width = masked_b.shape[1]
    own_width = c_width // 2
    own_b = lax.dynamic_slice_in_dim(masked_b, layer_index * own_width, own_width, 1)
    column_b = gather_directly(own_b, "row", 0)
    row_count = a_blocks.shape[0]
    block_rows = a_mask.shape[0]
    inner_local = a_mask.shape[1]
    inner_total = column_b.shape[0] // BS
    stacked_b = column_b.reshape(inner_total, BS, own_width)
    packed, codes = pack_blocks(a_blocks, a_mask)
    slot_count = packed.shape[0]
    row_ids = jnp.arange(block_rows, dtype=jnp.int32)
    blocks = lax.all_gather(packed, "col", axis=0, tiled=True)
    block_codes = lax.all_gather(codes, "col", axis=0, tiled=True)
    item_count = blocks.shape[0]
    owner = jnp.arange(item_count, dtype=jnp.int32) // slot_count
    inner = (owner * inner_local + block_codes[:, 1]).astype(jnp.int32)
    picked = jnp.take(stacked_b, inner, axis=0)
    partial_blocks = jnp.einsum("sij,sjn->sin", blocks, picked, preferred_element_type=jnp.float32)
    selector = (block_codes[:, 0][:, None] == row_ids[None, :]).astype(jnp.float32)
    summed = jnp.einsum("sr,sin->rin", selector, partial_blocks)
    product = summed.reshape(row_count, own_width)
    return product.astype(jnp.bfloat16)


def solution(mesh):
    in_specs = (P("row", "col"), P("row", "col"), P("row", "col"), P("row", "col"))
    out_specs = P("row", ("col", "rep"))
    return jax.shard_map(
        per_device, mesh=mesh, in_specs=in_specs, out_specs=out_specs, check_vma=False
    )
```

profile of v0, /device:TPU:4, one launch (start us, length us, event | category | flops | bytes accessed | tf_op | source)
XLA Modules:
  0.0 90.8 jit_solution(8333974112397646809)
XLA Ops:
  6.5 0.0 copy-start.1
  6.5 0.0 copy-start
  6.5 0.0 all-gather.3.cloned.1.call-start
  6.5 0.7 compare_bitcast_fusion
  7.3 0.8 reduce-window.8
  8.1 1.7 %reshape_transpose_reshape.3 = bf16[8,65536]{1,0:T(8,128)(2,1)S(1)} reshape(bf16[2048,256]{1,0:T(8,128)(2,1)} %param.4) | data formatting | bytes 2097152 | tf_op jit(solution)/shard_map/reshape;transpose;reshape | solution.py:47
  9.8 0.1 convert_reduce_fusion
  9.9 0.4 convolution_convert_fusion
  10.4 0.7 copy.29
  11.1 0.0 all-gather.3.cloned.1.call-update
  11.1 0.0 copy-done.1
  11.2 0.3 mul.31
  11.5 0.1 copy.23
  11.6 0.0 copy-done
  11.6 0.1 dynamic-slice_multiply_fusion
  11.7 1.5 %broadcast_in_dim.29 = bf16[8,512,256]{2,1,0:T(8,128)(2,1)} broadcast(bf16[512,256]{1,0:T(8,128)(2,1)S(1)} %dynamic-slice_multiply_fusion), dimensions={1,2} | broadcast | bytes 2359296 | tf_op jit(solution)/shard_map/broadcast_in_dim | solution.py:12
  13.2 8.5 %all-to-all-start = ((bf16[8,512,256]{2,1,0:T(8,128)(2,1)}), bf16[8,512,256]{2,1,0:T(8,128)(2,1)S(1)}, u32[]{:S(2)}, u32[]{:S(2)}) async-start(bf16[8,512,256]{2,1,0:T(8,128)(2,1)} %broadcast_in_dim.29), calls=%async_computation | async-start | bytes 4194304 | tf_op jit(solution)/shard_map/all_to_all | solution.py:11
  21.6 0.1 copy.21
  21.7 15.4 %all-gather = s32[16,2,2]{2,1,0:T(2,128)S(1)} all-gather(s32[1,2,2]{2,1,0:T(2,128)S(1)} %pad_bitcast_fusion), channel_id=1, replica_groups=mesh['row'=8,'col'=16,'rep'=2] {'col'}, dimensions={0}, use_global_device_ids=true | all-gather | bytes 272 | tf_op jit(solution)/shard_map/all_gather | solution.py:81
  37.1 0.1 fusion.15
  37.2 0.1 copy.19
  37.3 0.1 copy.20
  37.4 35.4 %all-to-all-done = bf16[8,512,256]{2,1,0:T(8,128)(2,1)S(1)} async-done(((bf16[8,512,256]{2,1,0:T(8,128)(2,1)}), bf16[8,512,256]{2,1,0:T(8,128)(2,1)S(1)}, u32[]{:S(2)}, u32[]{:S(2)}) %all-to-all-start) | async-done | bytes 2097184 | tf_op jit(solution)/shard_map/all_to_all | solution.py:11
  72.8 2.8 %gather_fusion = bf16[32,256,256]{2,1,0:T(8,128)(2,1)} fusion(bf16[16,256,256]{2,1,0:T(8,128)(2,1)S(1)} %bitcast.28, s32[1024]{0:T(1024)S(1)} %pad_clamp_fusion), kind=kCustom, calls=%fused_computation | custom fusion | bytes 8388736 | tf_op jit(solution)/shard_map/jit(_take)/gather | solution.py:85
  75.6 0.0 all-gather.3.cloned.1.call-done
  75.6 4.8 %fusion.2 = bf16[32,256,256]{2,1,0:T(8,128)(2,1)S(1)} fusion(bf16[32,256,256]{2,1,0:T(8,128)(2,1)} %all-gather.3.cloned.1.call-done, bf16[32,256,256]{2,1,0:T(8,128)(2,1)} %gather_fusion, pred[32]{0:T(512)(128)(4,1)S(1)} %get-tuple-element.7), kind=kOutput, calls=%fused_computation.4 | convolution fusion | flops 1075838976 | bytes 12582944 | tf_op jit(solution)/shard_map/sij,sjn->sin/dot_general | solution.py:86
  80.4 2.4 %fusion.6 = bf16[8,256,256]{2,0,1:T(8,128)(2,1)S(1)} fusion(bf16[32,256,256]{2,1,0:T(8,128)(2,1)S(1)} %fusion.2, s32[32]{0:T(128)S(1)} %bitcast.34), kind=kOutput, calls=%fused_computation.8 | convolution fusion | flops 33554688 | bytes 5243008 | tf_op jit(solution)/shard_map/sr,sin->rin/dot_general | solution.py:88
  82.8 1.2 %copy.17 = bf16[8,256,256]{2,1,0:T(8,128)(2,1)} copy(bf16[8,256,256]{2,0,1:T(8,128)(2,1)S(1)} %fusion.6) | data formatting | bytes 2097152 | tf_op jit(solution)/shard_map/convert_element_type | solution.py:90
  (6 shorter events, 0.0 us)
Async XLA Ops:
  6.5 4.6 %copy-start.1 = (s32[2,2]{1,0:T(2,128)S(1)}, s32[2,2]{1,0:T(2,128)}, u32[]{:S(2)}) copy-start(s32[2,2]{1,0:T(2,128)} %param.7) | copy-start | bytes 52
  6.5 5.1 %copy-start = (bf16[512,512]{1,0:T(8,128)(2,1)S(1)}, bf16[512,512]{1,0:T(8,128)(2,1)}, u32[]{:S(2)}) copy-start(bf16[512,512]{1,0:T(8,128)(2,1)} %param.6) | copy-start | bytes 1572868
  6.5 69.1 %all-gather.3.cloned.1.call-start = ((), (), s32[]{:S(2)}) async-start(), calls=%async_computation.1 | async-start | bytes 4456448 | tf_op jit(solution)/shard_map/all_gather | solution.py:80
  13.2 59.7 %all-to-all-start = ((bf16[8,512,256]{2,1,0:T(8,128)(2,1)}), bf16[8,512,256]{2,1,0:T(8,128)(2,1)S(1)}, u32[]{:S(2)}, u32[]{:S(2)}) async-start(bf16[8,512,256]{2,1,0:T(8,128)(2,1)} %broadcast_in_dim.29), calls=%async_computation | async-start | bytes 4194304 | tf_op jit(solution)/shard_map/all_to_all | solution.py:11
Sparse Core Ops, SparseCore 0:
  11.3 41.8 all-gather.2
where the time goes:
time: 91 us; the launch traced here: 90.8 us
  waiting for transfers between devices  35.4 us (39%)
  blocking collectives  15.4 us (17%)
  between operations  13.5 us (15%)
  local copies, waits for them, and re-layouts  8.6 us (9%)
  starting transfers between devices  8.47 us (9%)
  matrix products  7.58 us (8%)
  other arithmetic  1.81 us (2%)
    all_to_all x1, waiting for transfers between devices, from_everyone(): lax.all_to_all(jnp.broadcast_to(shard[None], (length, *shard.shape)), axi...  35.4 us
    all_gather x1, blocking collectives, per_device(): block_codes = lax.all_gather(codes, 'col', axis=0, tiled=True)  15.4 us
    all_to_all x1, starting transfers between devices, from_everyone(): lax.all_to_all(jnp.broadcast_to(shard[None], (length, *shard.shape)), axi...  8.47 us
    dot_general x1, matrix products, per_device(): jnp.einsum('sij,sjn->sin', blocks, picked, preferred_element_type=jnp.flo...  4.8 us
    gather x1, local copies, waits for them, and re-layouts, per_device(): picked = jnp.take(stacked_b, inner, axis=0)  2.77 us
    dot_general x1, matrix products, per_device(): summed = jnp.einsum('sr,sin->rin', selector, partial_blocks)  2.35 us
  transfers between devices with their start and end apart: 2, of which 1 were waited for; matrix products, arithmetic and copies ran while one was open for 6% of the time, Pallas kernels for 0%

commit v1 on v0

v1 whole, which is shorter than its diff:
```python
import functools

import jax
import jax.numpy as jnp
from jax import lax
from jax.experimental import pallas as pl
from jax.experimental.pallas import tpu as pltpu
from jax.sharding import PartitionSpec as P

BS = 256
CODE = 16
NCHUNK = 4
MESH = pl.DeviceIdType.MESH


def kernel(
    nz, nx, rows,
    a_ref, am_ref, b_ref, bm_ref, c_ref,
    avm, bvm, abuf, bbuf, dense, acc,
    load_sem, ax_send, ay_send, ad_send, a_recv, b_send, b_recv,
):
    z = lax.axis_index("row")
    col = lax.axis_index("col")
    rep = lax.axis_index("rep")
    x = col // 4
    yl = (col // 2) % 2
    core = col % 2
    width = BS
    chunk = b_ref.shape[0] // NCHUNK

    zr, zl = (z + 1) % nz, (z + nz - 1) % nz
    dev_zr, dev_zl = {"row": zr}, {"row": zl}

    def col_of(xx, yy, cc):
        return xx * 4 + yy * 2 + cc

    xs = [x, (x + nx - 1) % nx, (x + 1) % nx, (x + 2) % nx]
    dev_xr = {"col": col_of(xs[2], yl, core)}
    dev_xl = {"col": col_of(xs[1], yl, core)}
    dev_y = [
        {"col": col_of(x, 1 - yl, core), "rep": rep},
        {"col": col_of(x, 1 - yl, core), "rep": 1 - rep},
    ]
    dev_d = {"col": col_of(x, yl, 1 - core)}
    peers = [dev_zr, dev_zl, dev_xr, dev_xl, dev_y[0], dev_y[1], dev_d]

    load_b = [
        pltpu.make_async_copy(
            b_ref.at[pl.ds(j * chunk, chunk), pl.ds(pl.multiple_of(rep * width, width), width)],
            bvm.at[pl.ds(j * chunk, chunk)],
            load_sem.at[j],
        )
        for j in range(NCHUNK)
    ]
    load_a = pltpu.make_async_copy(a_ref, avm, load_sem.at[NCHUNK])
    for copy in load_b:
        copy.start()
    load_a.start()

    barrier = pltpu.get_barrier_semaphore()
    for peer in peers:
        pl.semaphore_signal(barrier, inc=1, device_id=peer, device_id_type=MESH)

    def b_copy(source, j, way, hop):
        piece = bbuf.at[source, pl.ds(j * chunk, chunk)]
        return pltpu.make_async_remote_copy(
            src_ref=piece,
            dst_ref=piece,
            send_sem=b_send.at[way, hop, j],
            recv_sem=b_recv.at[source, j],
            device_id=(dev_zr, dev_zl)[way],
            device_id_type=MESH,
        )

    def a_copy(item, slot, sem, dev):
        piece = abuf.at[2 * item + slot]
        return pltpu.make_async_remote_copy(
            src_ref=piece,
            dst_ref=piece,
            send_sem=sem,
            recv_sem=a_recv.at[2 * item + slot],
            device_id=dev,
            device_id_type=MESH,
        )

    sent = []

    def go(copy):
        copy.start()
        sent.append(copy)

    for j in range(NCHUNK):
        load_b[j].wait()
        keep = jnp.full((chunk, width), bm_ref[(j * chunk) // BS, rep].astype(jnp.float32))
        part = bvm[pl.ds(j * chunk, chunk), :]
        bbuf[z, pl.ds(j * chunk, chunk), :] = part * keep.astype(jnp.bfloat16)

    count = jnp.int32(0)
    lines = lax.broadcasted_iota(jnp.int32, (CODE, BS), 0)
    code = [jnp.zeros((CODE, BS), jnp.float32)] * 2
    weights = []
    for i in range(rows):
        m = am_ref[0, i]
        later = jnp.minimum(count, 1)
        count = count + m
        pair = [jnp.full((CODE, BS), (m * w).astype(jnp.float32)) for w in (1 - later, later)]
        code = [c + jnp.where(lines == i, p, 0.0) for c, p in zip(code, pair)]
        weights.append([p.astype(jnp.bfloat16) for p in pair])
    load_a.wait()

    def pack(t, _):
        at = pl.multiple_of(t * CODE, CODE)
        total = [None, None]
        for i in range(rows):
            part = avm[pl.ds(at + i * BS, CODE), :]
            for slot in range(2):
                term = part * weights[i][slot]
                total[slot] = term if i == 0 else total[slot] + term
        for slot in range(2):
            abuf[2 * col + slot, pl.ds(at, CODE), :] = total[slot]
        return 0

    lax.fori_loop(0, BS // CODE, pack, 0)
    for slot in range(2):
        abuf[2 * col + slot, pl.ds(BS, CODE), :] = code[slot].astype(jnp.bfloat16)

    pl.semaphore_wait(barrier, len(peers))

    def y_send(n, item, slot):
        go(a_copy(item, slot, ay_send.at[2 * n + slot], dev_y[slot]))

    def d_send(n, item, slot):
        go(a_copy(item, slot, ad_send.at[2 * n + slot], dev_d))

    def a_wait(item, slot):
        a_copy(item, slot, ad_send.at[0], dev_d).wait_recv()

    mine = [col_of(xx, yl, core) for xx in xs]
    other = [col_of(xx, 1 - yl, core) for xx in xs]

    def b_step(hop, j):
        if hop < nz // 2 or j < NCHUNK // 2:
            source = (z + nz - hop) % nz
            b_copy(source, j, 0, 0).wait_recv()
            if hop + 1 < nz // 2 or (hop + 1 == nz // 2 and j < NCHUNK // 2):
                go(b_copy(source, j, 0, hop))
        if hop < nz // 2 or j >= NCHUNK // 2:
            source = (z + hop) % nz
            b_copy(source, j, 1, 0).wait_recv()
            if hop + 1 < nz // 2 or (hop + 1 == nz // 2 and j >= NCHUNK // 2):
                go(b_copy(source, j, 1, hop))

    for j in range(NCHUNK):
        go(b_copy(z, j, 0, 0))
        go(b_copy(z, j, 1, 0))
        if j < 2:
            go(a_copy(col, j, ax_send.at[j], dev_xr))
            go(a_copy(col, j, ax_send.at[2 + j], dev_xl))
            y_send(0, col, j)
    for slot in range(2):
        d_send(0, col, slot)

    def x_arrival(slot):
        for n in (1, 2):
            a_wait(mine[n], slot)
            y_send(n, mine[n], slot)
            if slot == n - 1:
                go(a_copy(mine[n], slot, ax_send.at[3 + n], (dev_xr, dev_xl)[slot]))
            d_send(n, mine[n], slot)

    def y_arrival(n, slot):
        a_wait(other[n], slot)
        d_send(4 + n, other[n], slot)

    def expand(xx, yy):
        def body(r, _):
            for cc in range(2):
                k = col_of(xx, yy, cc)
                total = None
                for slot in range(2):
                    row = abuf[2 * k + slot, pl.ds(BS, CODE), :].astype(jnp.float32)
                    at = lax.broadcasted_iota(jnp.int32, (CODE, BS), 0) == r
                    row = jnp.sum(jnp.where(at, row, 0.0), axis=0, keepdims=True)
                    row = jnp.broadcast_to(row, (CODE, BS)).astype(jnp.bfloat16)
                    block = abuf[2 * k + slot, pl.ds(0, BS), :].reshape(BS // CODE, CODE, BS)
                    term = block * row[None]
                    total = term if total is None else total + term
                dense[xx * 2 + yy, pl.ds(pl.multiple_of(r * BS, BS), BS), pl.ds(cc * BS, BS)] = total.reshape(BS, BS)
            return 0

        lax.fori_loop(0, rows, body, 0)

    def d_arrival(n, yy):
        for slot in range(2):
            a_wait(col_of(xs[n], yy, 1 - core), slot)
        expand(xs[n], yy)

    b_step(1, 0)
    x_arrival(0)
    y_arrival(0, 0)
    b_step(1, 1)
    y_arrival(0, 1)
    b_step(1, 2)
    x_arrival(1)
    b_step(1, 3)
    d_arrival(0, yl)
    b_step(2, 0)
    for slot in range(2):
        a_wait(mine[3], slot)
        y_send(3, mine[3], slot)
        d_send(3, mine[3], slot)
    d_arrival(0, 1 - yl)
    y_arrival(1, 0)
    y_arrival(2, 0)
    b_step(2, 1)
    d_arrival(1, yl)
    b_step(2, 2)
    y_arrival(1, 1)
    y_arrival(2, 1)
    d_arrival(2, yl)
    b_step(2, 3)
    d_arrival(3, yl)
    b_step(3, 0)
    for slot in range(2):
        y_arrival(3, slot)
    d_arrival(1, 1 - yl)
    d_arrival(2, 1 - yl)
    b_step(3, 1)
    d_arrival(3, 1 - yl)

    tile = 2 * BS

    def multiply(source, start):
        def body(t, _):
            at = pl.ds(pl.multiple_of(t * tile, tile), tile)
            total = jnp.dot(dense[source, at, :], bbuf[source], preferred_element_type=jnp.float32)
            if start:
                acc[at, :] = total
            else:
                acc[at, :] += total
            return 0

        lax.fori_loop(0, rows * BS // tile, body, 0)

    multiply(z, True)
    multiply((z + 1) % nz, False)
    multiply((z + nz - 1) % nz, False)
    b_step(3, 2)
    multiply((z + 2) % nz, False)
    b_step(3, 3)
    multiply((z + nz - 2) % nz, False)
    multiply((z + 3) % nz, False)
    multiply((z + nz - 3) % nz, False)
    for j in range(NCHUNK):
        b_step(nz // 2, j)
    last = (z + nz // 2) % nz

    def finish(t, _):
        at = pl.ds(pl.multiple_of(t * tile, tile), tile)
        total = jnp.dot(dense[last, at, :], bbuf[last], preferred_element_type=jnp.float32)
        c_ref[at, :] = (acc[at, :] + total).astype(jnp.bfloat16)
        return 0

    lax.fori_loop(0, rows * BS // tile, finish, 0)
    for copy in sent:
        copy.wait_send()


def solution(mesh):
    nz = mesh.shape["row"]
    nx = mesh.shape["col"] // 4

    def per_device(a, am, b, bm):
        rows = am.shape[0]
        ncol = nx * 4
        depth = b.shape[0]
        width = b.shape[1] // 2
        return pl.pallas_call(
            functools.partial(kernel, nz, nx, rows),
            out_shape=jax.ShapeDtypeStruct((a.shape[0], width), jnp.bfloat16),
            in_specs=[
                pl.BlockSpec(memory_space=pltpu.HBM),
                pl.BlockSpec(memory_space=pltpu.SMEM),
                pl.BlockSpec(memory_space=pltpu.HBM),
                pl.BlockSpec(memory_space=pltpu.SMEM),
            ],
            out_specs=pl.BlockSpec(memory_space=pltpu.VMEM),
            scratch_shapes=[
                pltpu.VMEM(a.shape, jnp.bfloat16),
                pltpu.VMEM((depth, width), jnp.bfloat16),
                pltpu.VMEM((2 * ncol, BS + CODE, BS), jnp.bfloat16),
                pltpu.VMEM((nz, depth, width), jnp.bfloat16),
                pltpu.VMEM((nz, a.shape[0], 2 * BS), jnp.bfloat16),
                pltpu.VMEM((a.shape[0], width), jnp.float32),
                pltpu.SemaphoreType.DMA((NCHUNK + 1,)),
                pltpu.SemaphoreType.DMA((6,)),
                pltpu.SemaphoreType.DMA((8,)),
                pltpu.SemaphoreType.DMA((16,)),
                pltpu.SemaphoreType.DMA((2 * ncol,)),
                pltpu.SemaphoreType.DMA((2, 4, NCHUNK)),
                pltpu.SemaphoreType.DMA((nz, NCHUNK)),
            ],
            compiler_params=pltpu.CompilerParams(
                collective_id=0, has_side_effects=True, vmem_limit_bytes=40 * 2**20
            ),
        )(a, am.reshape(1, rows), b, bm)

    spec = P("row", "col")
    return jax.shard_map(
        per_device,
        mesh=mesh,
        in_specs=(spec, spec, spec, spec),
        out_specs=P("row", ("col", "rep")),
        check_vma=False,
    )
```

time: 91 us -> 45.1 us (0.50)
  the two profiles are of different devices: /device:TPU:4 before, /device:TPU:1 now
where the time goes in v1:
time: 45.1 us; the launch traced here: 44.9 us
  Pallas kernels  41 us (91%)
  local copies, waits for them, and re-layouts  3.92 us (9%)
    pallas_call x1, Pallas kernels, per_device(): pl.pallas_call(functools.partial(kernel, nz, nx, rows), out_shape=jax.Sha...  41 us
    unnamed x9, local copies, waits for them, and re-layouts  3.92 us

profile of v1, /device:TPU:1, one launch (start us, length us, event | category | flops | bytes accessed | tf_op | source)
XLA Modules:
  0.0 44.9 jit_solution(4409306463023797649)
XLA Ops:
  0.0 0.0 copy-start.2
  0.0 0.0 copy-start.3
  0.0 0.7 %copy-done.2 = s32[2,2]{1,0:T(2,128)S(1)} copy-done((s32[2,2]{1,0:T(2,128)S(1)}, s32[2,2]{1,0:T(2,128)}, u32[]{:S(2)}) %copy-start.2) | copy-done | bytes 40
  0.7 0.0 copy-done.3
  0.7 0.0 copy-start
  0.7 1.2 %copy-done = bf16[2048,256]{1,0:T(8,128)(2,1)S(1)} copy-done((bf16[2048,256]{1,0:T(8,128)(2,1)S(1)}, bf16[2048,256]{1,0:T(8,128)(2,1)}, u32[]{:S(2)}) %copy-start) | copy-done | bytes 1048600
  1.9 0.0 copy-start.1
  1.9 1.0 %copy-done.1 = bf16[512,512]{1,0:T(8,128)(2,1)S(1)} copy-done((bf16[512,512]{1,0:T(8,128)(2,1)S(1)}, bf16[512,512]{1,0:T(8,128)(2,1)}, u32[]{:S(2)}) %copy-start.1) | copy-done | bytes 524312
  3.0 41.0 %shard_map.46 = bf16[2048,256]{1,0:T(8,128)(2,1)S(1)} custom-call(bf16[2048,256]{1,0:T(8,128)(2,1)S(1)} %copy-done, s32[1,8]{1,0:T(1,128)S(1)} %bitcast.1, bf16[512,512]{1,0:T(8,128)(2,1)S(1)} %copy-done.1, s32[2,2]{1,0:T(2,128)S(1)} %copy-done.2), custom_call_target="tpu_custom_call" | custom-call | tf_op jit(solution)/shard_map/pallas_call | solution.py:278
  43.9 1.0 %copy.6 = bf16[2048,256]{1,0:T(8,128)(2,1)} copy(bf16[2048,256]{1,0:T(8,128)(2,1)S(1)} %shard_map.46) | data formatting | bytes 2097152
Async XLA Ops:
  0.0 0.7 %copy-start.2 = (s32[2,2]{1,0:T(2,128)S(1)}, s32[2,2]{1,0:T(2,128)}, u32[]{:S(2)}) copy-start(s32[2,2]{1,0:T(2,128)} %bm_ref.1) | copy-start | bytes 52
  0.0 0.7 %copy-start.3 = (s32[8,1]{0,1:T(1,128)S(1)}, s32[8,1]{0,1:T(1,128)}, u32[]{:S(2)}) copy-start(s32[8,1]{0,1:T(1,128)} %param.5) | copy-start | bytes 100
  0.7 1.2 %copy-start = (bf16[2048,256]{1,0:T(8,128)(2,1)S(1)}, bf16[2048,256]{1,0:T(8,128)(2,1)}, u32[]{:S(2)}) copy-start(bf16[2048,256]{1,0:T(8,128)(2,1)} %a_ref.1) | copy-start | bytes 3145732
  1.9 1.0 %copy-start.1 = (bf16[512,512]{1,0:T(8,128)(2,1)S(1)}, bf16[512,512]{1,0:T(8,128)(2,1)}, u32[]{:S(2)}) copy-start(bf16[512,512]{1,0:T(8,128)(2,1)} %b_ref.1) | copy-start | bytes 1572868

commit v2 on v1

v2 whole, which is shorter than its diff:
```python
import functools

import jax
import jax.numpy as jnp
from jax import lax
from jax.experimental import pallas as pl
from jax.experimental.pallas import tpu as pltpu
from jax.sharding import PartitionSpec as P

BS = 256
HALF = BS // 2
TILE = 64
CODE = 16
CHUNKS = ((0, 128), (256, 128), (384, 128), (128, 128))
WAYS = (0, 1, 1, 0)
MESH = pl.DeviceIdType.MESH


def kernel(
    nz, nx, rows,
    a_ref, am_ref, b_ref, bm_ref, c_ref,
    avm, bvm, ams, bms, abuf, bbuf, dense, acc,
    load_sem, ax_send, ay_send, ad_send, a_recv, b_send, b_recv,
):
    z = lax.axis_index("row")
    col = lax.axis_index("col")
    rep = lax.axis_index("rep")
    x = col // 4
    yl = (col // 2) % 2
    core = col % 2
    width = BS
    far = nz // 2

    def col_of(xx, yy, cc):
        return xx * 4 + yy * 2 + cc

    xs = [x, (x + nx - 1) % nx, (x + 1) % nx, (x + 2) % nx]
    dev_z = ({"row": (z + 1) % nz}, {"row": (z + nz - 1) % nz})
    dev_x = ({"col": col_of(xs[2], yl, core)}, {"col": col_of(xs[1], yl, core)})
    dev_y = (
        {"col": col_of(x, 1 - yl, core), "rep": rep},
        {"col": col_of(x, 1 - yl, core), "rep": 1 - rep},
    )
    dev_d = {"col": col_of(x, yl, 1 - core)}
    peers = [*dev_z, *dev_x, *dev_y, dev_d]

    load_bm = pltpu.make_async_copy(bm_ref, bms, load_sem.at[0])
    load_am = pltpu.make_async_copy(am_ref, ams, load_sem.at[1])
    load_b = pltpu.make_async_copy(
        b_ref.at[:, pl.ds(pl.multiple_of(rep * width, width), width)], bvm, load_sem.at[2]
    )
    load_a = pltpu.make_async_copy(a_ref, avm, load_sem.at[3])
    for copy in (load_bm, load_b, load_am, load_a):
        copy.start()

    barrier = pltpu.get_barrier_semaphore()
    for peer in peers:
        pl.semaphore_signal(barrier, inc=1, device_id=peer, device_id_type=MESH)

    sent = []

    def go(copy):
        copy.start()
        sent.append(copy)

    def b_copy(source, j, way, hop):
        piece = bbuf.at[source, pl.ds(*CHUNKS[j])]
        return pltpu.make_async_remote_copy(
            src_ref=piece,
            dst_ref=piece,
            send_sem=b_send.at[way, hop, j],
            recv_sem=b_recv.at[source, j],
            device_id=dev_z[way],
            device_id_type=MESH,
        )

    def a_copy(item, slot, part, sem, dev):
        start, size = ((0, BS + CODE), (0, HALF), (HALF, HALF + CODE))[part]
        piece = abuf.at[2 * item + slot, pl.ds(start, size)]
        return pltpu.make_async_remote_copy(
            src_ref=piece,
            dst_ref=piece,
            send_sem=sem,
            recv_sem=a_recv.at[2 * item + slot, part],
            device_id=dev,
            device_id_type=MESH,
        )

    def b_step(hop, j):
        for way in range(2):
            if hop < far or WAYS[j] == way:
                source = ((z + nz - hop) % nz, (z + hop) % nz)[way]
                b_copy(source, j, way, 0).wait_recv()
                if hop + 1 < far or (hop + 1 == far and WAYS[j] == way):
                    go(b_copy(source, j, way, hop))

    def y_send(n, item, slot, part):
        link = (slot + part) % 2
        go(a_copy(item, slot, part, ay_send.at[4 * n + 2 * slot + part - 1], dev_y[link]))

    def d_send(n, item, slot):
        go(a_copy(item, slot, 0, ad_send.at[2 * n + slot], dev_d))

    def x_send(n, item, slot, part, way):
        go(a_copy(item, slot, part, ax_send.at[way, 4 * n + 2 * slot + part - 1], dev_x[way]))

    load_bm.wait()
    load_b.wait()
    for start, size in CHUNKS:
        keep = jnp.full((size, width), bms[start // BS, rep].astype(jnp.float32))
        bbuf[z, pl.ds(start, size), :] = bvm[pl.ds(start, size), :] * keep.astype(jnp.bfloat16)
    pl.semaphore_wait(barrier, len(peers))
    for j in range(len(CHUNKS)):
        for way in range(2):
            go(b_copy(z, j, way, 0))

    load_am.wait()
    count = jnp.int32(0)
    lines = lax.broadcasted_iota(jnp.int32, (CODE, BS), 0)
    code = [jnp.zeros((CODE, BS), jnp.float32)] * 2
    weights = []
    for i in range(rows):
        m = ams[0, i]
        later = jnp.minimum(count, 1)
        count = count + m
        pair = [jnp.full((CODE, BS), (m * w).astype(jnp.float32)) for w in (1 - later, later)]
        code = [c + jnp.where(lines == i, p, 0.0) for c, p in zip(code, pair)]
        weights.append([p.astype(jnp.bfloat16) for p in pair])
    load_a.wait()

    def pack(t, _):
        at = pl.multiple_of(t * 4 * CODE, 4 * CODE)
        total = [None, None]
        for i in range(rows):
            part = avm[pl.ds(at + i * BS, 4 * CODE), :].reshape(4, CODE, BS)
            for slot in range(2):
                term = part * weights[i][slot][None]
                total[slot] = term if i == 0 else total[slot] + term
        for slot in range(2):
            abuf[2 * col + slot, pl.ds(at, 4 * CODE), :] = total[slot].reshape(4 * CODE, BS)
        return 0

    lax.fori_loop(0, BS // (4 * CODE), pack, 0)
    for slot in range(2):
        abuf[2 * col + slot, pl.ds(BS, CODE), :] = code[slot].astype(jnp.bfloat16)
    for turn in range(4):
        for way in range(2):
            x_send(0, col, (turn // 2 + way) % 2, turn % 2 + 1, way)
        if turn < 2:
            for slot in range(2):
                y_send(0, col, slot, turn + 1)
    for slot in range(2):
        d_send(0, col, slot)

    mine = [col_of(xx, yl, core) for xx in xs]
    other = [col_of(xx, 1 - yl, core) for xx in xs]

    def a_wait(item, slot, part):
        a_copy(item, slot, part, ad_send.at[0], dev_d).wait_recv()

    def x_arrival(turn):
        part = turn % 2 + 1
        for n in (1, 2):
            slot = (turn // 2 + n - 1) % 2
            a_wait(mine[n], slot, part)
            y_send(n, mine[n], slot, part)
            if turn < 2:
                x_send(1, mine[n], slot, part, n - 1)
            if part == 2:
                d_send(n, mine[n], slot)

    def x_second(part):
        for slot in range(2):
            a_wait(mine[3], slot, part)
            if part == 1:
                y_send(3, mine[3], slot, part)
            else:
                d_send(3, mine[3], slot)

    def y_arrival(turn):
        part = turn % 2 + 1
        for n in (1, 2):
            slot = (turn // 2 + n - 1) % 2
            a_wait(other[n], slot, part)
            if part == 2:
                d_send(4 + n, other[n], slot)
                if slot == n - 1:
                    x_send(2, other[n], slot, 2, n - 1)

    def y_plain(n, part):
        for slot in range(2):
            a_wait(other[n], slot, part)
            if part == (1 if n else 2):
                d_send(4 + n, other[n], slot)

    def expand(n, yy):
        xx = xs[n]
        for slot in range(2):
            a_wait(col_of(xx, yy, 1 - core), slot, 0)

        weights = []
        for cc in range(2):
            for slot in range(2):
                line = abuf[2 * col_of(xx, yy, cc) + slot, pl.ds(BS, CODE), :].astype(jnp.float32)
                weights.append(
                    [jnp.broadcast_to(line[r : r + 1], (CODE, BS)).astype(jnp.bfloat16)[None] for r in range(rows)]
                )

        def body(t, _):
            at = pl.multiple_of(t * TILE, TILE)
            for cc in range(2):
                k = col_of(xx, yy, cc)
                one, two = (
                    abuf[2 * k + slot, pl.ds(at, TILE), :].reshape(TILE // CODE, CODE, BS) for slot in range(2)
                )
                for r in range(rows):
                    total = one * weights[2 * cc][r] + two * weights[2 * cc + 1][r]
                    dense[xx * 2 + yy, pl.ds(at + r * BS, TILE), pl.ds(cc * BS, BS)] = total.reshape(TILE, BS)
            return 0

        lax.fori_loop(0, BS // TILE, body, 0)

    def multiply(source, first=False):
        total = jnp.dot(dense[source], bbuf[source], preferred_element_type=jnp.float32)
        acc[...] = total if first else acc[...] + total

    expand(0, yl)
    b_step(1, 0)
    x_arrival(0)
    y_plain(0, 1)
    b_step(1, 1)
    x_arrival(1)
    y_plain(0, 2)
    b_step(1, 2)
    x_arrival(2)
    expand(0, 1 - yl)
    b_step(1, 3)
    y_arrival(0)
    x_arrival(3)
    b_step(2, 0)
    y_arrival(1)
    x_second(1)
    expand(1, yl)
    b_step(2, 1)
    y_arrival(2)
    x_second(2)
    expand(2, yl)
    b_step(2, 2)
    y_arrival(3)
    expand(3, yl)
    b_step(2, 3)
    expand(1, 1 - yl)
    y_plain(3, 2)
    y_plain(3, 1)
    expand(2, 1 - yl)
    b_step(3, 0)
    expand(3, 1 - yl)
    b_step(3, 1)
    multiply(z, True)
    b_step(3, 2)
    multiply((z + 1) % nz)
    b_step(3, 3)
    multiply((z + nz - 1) % nz)
    multiply((z + 2) % nz)
    multiply((z + nz - 2) % nz)
    multiply((z + 3) % nz)
    multiply((z + nz - 3) % nz)
    for j in range(len(CHUNKS)):
        b_step(far, j)
    last = (z + far) % nz
    total = jnp.dot(dense[last], bbuf[last], preferred_element_type=jnp.float32)
    c_ref[...] = (acc[...] + total).astype(jnp.bfloat16)
    for copy in sent:
        copy.wait_send()


def solution(mesh):
    nz = mesh.shape["row"]
    nx = mesh.shape["col"] // 4

    def per_device(a, am, b, bm):
        rows = am.shape[0]
        ncol = nx * 4
        depth = b.shape[0]
        width = b.shape[1] // 2
        am = am.reshape(1, rows)
        return pl.pallas_call(
            functools.partial(kernel, nz, nx, rows),
            out_shape=jax.ShapeDtypeStruct((a.shape[0], width), jnp.bfloat16),
            in_specs=[pl.BlockSpec(memory_space=pl.ANY)] * 4,
            out_specs=pl.BlockSpec(memory_space=pltpu.VMEM),
            scratch_shapes=[
                pltpu.VMEM(a.shape, jnp.bfloat16),
                pltpu.VMEM((depth, width), jnp.bfloat16),
                pltpu.SMEM(am.shape, jnp.int32),
                pltpu.SMEM(bm.shape, jnp.int32),
                pltpu.VMEM((2 * ncol, BS + CODE, BS), jnp.bfloat16),
                pltpu.VMEM((nz, depth, width), jnp.bfloat16),
                pltpu.VMEM((nz, a.shape[0], 2 * BS), jnp.bfloat16),
                pltpu.VMEM((a.shape[0], width), jnp.float32),
                pltpu.SemaphoreType.DMA((4,)),
                pltpu.SemaphoreType.DMA((2, 12)),
                pltpu.SemaphoreType.DMA((16,)),
                pltpu.SemaphoreType.DMA((16,)),
                pltpu.SemaphoreType.DMA((2 * ncol, 3)),
                pltpu.SemaphoreType.DMA((2, nz // 2, len(CHUNKS))),
                pltpu.SemaphoreType.DMA((nz, len(CHUNKS))),
            ],
            compiler_params=pltpu.CompilerParams(
                collective_id=0, has_side_effects=True, vmem_limit_bytes=58 * 2**20
            ),
        )(a, am, b, bm)

    spec = P("row", "col")
    return jax.shard_map(
        per_device,
        mesh=mesh,
        in_specs=(spec, spec, spec, spec),
        out_specs=P("row", ("col", "rep")),
        check_vma=False,
    )
```

time: 45.1 us -> 38.8 us (0.86)
  Pallas kernels: 41 us -> 36.4 us
  local copies, waits for them, and re-layouts: 3.92 us -> 2.26 us
    pallas_call x1, Pallas kernels: 41 us -> 36.4 us  [per_device(): pl.pallas_call(functools.partial(kernel, nz, nx, rows), out_shape=jax.Sha...]
    unnamed x9 -> x1, local copies, waits for them, and re-layouts: 3.92 us -> 2.26 us
where the time goes in v2:
time: 38.8 us; the launch traced here: 38.7 us
  Pallas kernels  36.4 us (94%)
  local copies, waits for them, and re-layouts  2.26 us (6%)
    pallas_call x1, Pallas kernels, per_device(): pl.pallas_call(functools.partial(kernel, nz, nx, rows), out_shape=jax.Sha...  36.4 us
    unnamed x1, local copies, waits for them, and re-layouts  2.26 us

profile of v2, /device:TPU:1, one launch (start us, length us, event | category | flops | bytes accessed | tf_op | source)
XLA Modules:
  0.0 38.7 jit_solution(18302767961295436283)
XLA Ops:
  0.0 36.4 %shard_map.46 = bf16[2048,256]{1,0:T(8,128)(2,1)} custom-call(bf16[2048,256]{1,0:T(8,128)(2,1)} %a_ref.1, s32[1,8]{1,0:T(1,128)} %bitcast.1, bf16[512,512]{1,0:T(8,128)(2,1)} %b_ref.1, s32[2,2]{1,0:T(2,128)} %bm_ref.1), custom_call_target="tpu_custom_call" | custom-call | tf_op jit(solution)/shard_map/pallas_call | solution.py:287
  36.4 2.3 %copy.6 = bf16[2048,256]{1,0:T(8,128)(2,1)} copy(bf16[2048,256]{1,0:T(8,128)(2,1)} %shard_map.46) | data formatting | bytes 2097152

commit v3 on v2

--- a/solution.py
+++ b/solution.py
@@ -13,6 +13,7 @@
 CODE = 16
 CHUNKS = ((0, 128), (256, 128), (384, 128), (128, 128))
 WAYS = (0, 1, 1, 0)
+X_FIRST, X_FAR, Y_OWN, Y_FIRST, Y_FAR, D_FIRST = 0, 4, 6, 8, 12, 14
 MESH = pl.DeviceIdType.MESH
 
 
@@ -20,7 +21,7 @@
     nz, nx, rows,
     a_ref, am_ref, b_ref, bm_ref, c_ref,
     avm, bvm, ams, bms, abuf, bbuf, dense, acc,
-    load_sem, ax_send, ay_send, ad_send, a_recv, b_send, b_recv,
+    load_sem, a_send, a_recv, b_send, b_recv,
 ):
     z = lax.axis_index("row")
     col = lax.axis_index("col")
@@ -57,52 +58,44 @@
     for peer in peers:
         pl.semaphore_signal(barrier, inc=1, device_id=peer, device_id_type=MESH)
 
-    sent = []
-
-    def go(copy):
-        copy.start()
-        sent.append(copy)
-
-    def b_copy(source, j, way, hop):
-        piece = bbuf.at[source, pl.ds(*CHUNKS[j])]
+    def remote(piece, send_sem, recv_sem, dev):
         return pltpu.make_async_remote_copy(
             src_ref=piece,
             dst_ref=piece,
-            send_sem=b_send.at[way, hop, j],
-            recv_sem=b_recv.at[source, j],
-            device_id=dev_z[way],
-            device_id_type=MESH,
-        )
-
-    def a_copy(item, slot, part, sem, dev):
-        start, size = ((0, BS + CODE), (0, HALF), (HALF, HALF + CODE))[part]
-        piece = abuf.at[2 * item + slot, pl.ds(start, size)]
-        return pltpu.make_async_remote_copy(
-            src_ref=piece,
-            dst_ref=piece,
-            send_sem=sem,
-            recv_sem=a_recv.at[2 * item + slot, part],
+            send_sem=send_sem,
+            recv_sem=recv_sem,
             device_id=dev,
             device_id_type=MESH,
         )
 
+    def b_send_to(source, j, way, hop):
+        sem = b_recv.at[(hop - 1) * len(CHUNKS) + j if hop < far else (far - 1) * len(CHUNKS)]
+        remote(bbuf.at[source, pl.ds(*CHUNKS[j])], b_send, sem, dev_z[way]).start()
+
+    def b_wait(sem, lines):
+        remote(bbuf.at[z, pl.ds(0, lines)], b_send, sem, dev_z[0]).wait_recv()
+
     def b_step(hop, j):
+        b_wait(b_recv.at[(hop - 1) * len(CHUNKS) + j], 2 * CHUNKS[j][1])
         for way in range(2):
-            if hop < far or WAYS[j] == way:
-                source = ((z + nz - hop) % nz, (z + hop) % nz)[way]
-                b_copy(source, j, way, 0).wait_recv()
-                if hop + 1 < far or (hop + 1 == far and WAYS[j] == way):
-                    go(b_copy(source, j, way, hop))
-
-    def y_send(n, item, slot, part):
-        link = (slot + part) % 2
-        go(a_copy(item, slot, part, ay_send.at[4 * n + 2 * slot + part - 1], dev_y[link]))
+            if hop + 1 < far or WAYS[j] == way:
+                b_send_to(((z + nz - hop) % nz, (z + hop) % nz)[way], j, way, hop + 1)
+
+    def a_send_to(item, slot, part, sem, dev):
+        start, size = ((0, BS + CODE), (0, HALF), (HALF, HALF + CODE))[part]
+        remote(abuf.at[2 * item + slot, pl.ds(start, size)], a_send, a_recv.at[sem], dev).start()
+
+    def y_send(item, slot, part, sem):
+        a_send_to(item, slot, part, sem, dev_y[(slot + part) % 2])
 
     def d_send(n, item, slot):
-        go(a_copy(item, slot, 0, ad_send.at[2 * n + slot], dev_d))
-
-    def x_send(n, item, slot, part, way):
-        go(a_copy(item, slot, part, ax_send.at[way, 4 * n + 2 * slot + part - 1], dev_x[way]))
+        a_send_to(item, slot, 0, D_FIRST + n, dev_d)
+
+    def x_send(item, slot, part, way, sem):
+        a_send_to(item, slot, part, sem, dev_x[way])
+
+    def a_wait(sem, part):
+        b_wait(a_recv.at[sem], 2 * (0, HALF, HALF + CODE)[part])
 
     load_bm.wait()
     load_b.wait()
@@ -112,7 +105,7 @@
     pl.semaphore_wait(barrier, len(peers))
     for j in range(len(CHUNKS)):
         for way in range(2):
-            go(b_copy(z, j, way, 0))
+            b_send_to(z, j, way, 1)
 
     load_am.wait()
     count = jnp.int32(0)
@@ -145,58 +138,61 @@
         abuf[2 * col + slot, pl.ds(BS, CODE), :] = code[slot].astype(jnp.bfloat16)
     for turn in range(4):
         for way in range(2):
-            x_send(0, col, (turn // 2 + way) % 2, turn % 2 + 1, way)
+            x_send(col, (turn // 2 + way) % 2, turn % 2 + 1, way, X_FIRST + turn)
         if turn < 2:
             for slot in range(2):
-                y_send(0, col, slot, turn + 1)
+                y_send(col, slot, turn + 1, Y_OWN + turn)
     for slot in range(2):
         d_send(0, col, slot)
 
     mine = [col_of(xx, yl, core) for xx in xs]
     other = [col_of(xx, 1 - yl, core) for xx in xs]
 
-    def a_wait(item, slot, part):
-        a_copy(item, slot, part, ad_send.at[0], dev_d).wait_recv()
-
     def x_arrival(turn):
         part = turn % 2 + 1
+        a_wait(X_FIRST + turn, part)
         for n in (1, 2):
             slot = (turn // 2 + n - 1) % 2
-            a_wait(mine[n], slot, part)
-            y_send(n, mine[n], slot, part)
+            y_send(mine[n], slot, part, Y_FIRST + turn)
             if turn < 2:
-                x_send(1, mine[n], slot, part, n - 1)
+                x_send(mine[n], slot, part, n - 1, X_FAR + turn)
             if part == 2:
                 d_send(n, mine[n], slot)
 
     def x_second(part):
+        a_wait(X_FAR + part - 1, part)
         for slot in range(2):
-            a_wait(mine[3], slot, part)
             if part == 1:
-                y_send(3, mine[3], slot, part)
+                y_send(mine[3], slot, part, Y_FAR)
             else:
                 d_send(3, mine[3], slot)
 
+    def y_own():
+        for part in (1, 2):
+            a_wait(Y_OWN + part - 1, part)
+        for slot in range(2):
+            d_send(4, other[0], slot)
+
     def y_arrival(turn):
         part = turn % 2 + 1
-        for n in (1, 2):
-            slot = (turn // 2 + n - 1) % 2
-            a_wait(other[n], slot, part)
-            if part == 2:
+        a_wait(Y_FIRST + turn, part)
+        if part == 2:
+            for n in (1, 2):
+                slot = (turn // 2 + n - 1) % 2
+                if slot == n - 1:
+                    x_send(other[n], slot, part, n - 1, Y_FAR + 1)
                 d_send(4 + n, other[n], slot)
-                if slot == n - 1:
-                    x_send(2, other[n], slot, 2, n - 1)
-
-    def y_plain(n, part):
+
+    def y_far():
+        for part in (2, 1):
+            a_wait(Y_FAR + part - 1, part)
         for slot in range(2):
-            a_wait(other[n], slot, part)
-            if part == (1 if n else 2):
-                d_send(4 + n, other[n], slot)
-
-    def expand(n, yy):
+            d_send(7, other[3], slot)
+
+    def expand(n, far_y):
         xx = xs[n]
-        for slot in range(2):
-            a_wait(col_of(xx, yy, 1 - core), slot, 0)
+        yy = 1 - yl if far_y else yl
+        remote(abuf.at[pl.ds(0, 2)], a_send, a_recv.at[D_FIRST + n + 4 * far_y], dev_d).wait_recv()
 
         weights = []
         for cc in range(2):
@@ -224,37 +220,35 @@
         total = jnp.dot(dense[source], bbuf[source], preferred_element_type=jnp.float32)
         acc[...] = total if first else acc[...] + total
 
-    expand(0, yl)
+    expand(0, 0)
     b_step(1, 0)
     x_arrival(0)
-    y_plain(0, 1)
     b_step(1, 1)
     x_arrival(1)
-    y_plain(0, 2)
+    y_own()
     b_step(1, 2)
     x_arrival(2)
-    expand(0, 1 - yl)
+    expand(0, 1)
     b_step(1, 3)
     y_arrival(0)
     x_arrival(3)
     b_step(2, 0)
     y_arrival(1)
     x_second(1)
-    expand(1, yl)
+    expand(1, 0)
     b_step(2, 1)
     y_arrival(2)
     x_second(2)
-    expand(2, yl)
+    expand(2, 0)
     b_step(2, 2)
     y_arrival(3)
-    expand(3, yl)
+    expand(3, 0)
     b_step(2, 3)
-    expand(1, 1 - yl)
-    y_plain(3, 2)
-    y_plain(3, 1)
-    expand(2, 1 - yl)
+    expand(1, 1)
+    y_far()
+    expand(2, 1)
     b_step(3, 0)
-    expand(3, 1 - yl)
+    expand(3, 1)
     b_step(3, 1)
     multiply(z, True)
     b_step(3, 2)
@@ -265,13 +259,12 @@
     multiply((z + nz - 2) % nz)
     multiply((z + 3) % nz)
     multiply((z + nz - 3) % nz)
-    for j in range(len(CHUNKS)):
-        b_step(far, j)
+    b_wait(b_recv.at[(far - 1) * len(CHUNKS)], b_ref.shape[0])
     last = (z + far) % nz
     total = jnp.dot(dense[last], bbuf[last], preferred_element_type=jnp.float32)
     c_ref[...] = (acc[...] + total).astype(jnp.bfloat16)
-    for copy in sent:
-        copy.wait_send()
+    remote(bbuf.at[pl.ds(0, nz - 1)], b_send, b_recv.at[0], dev_z[0]).wait_send()
+    remote(abuf.at[pl.ds(0, 30)], a_send, a_recv.at[0], dev_d).wait_send()
 
 
 def solution(mesh):
@@ -299,17 +292,15 @@
                 pltpu.VMEM((nz, a.shape[0], 2 * BS), jnp.bfloat16),
                 pltpu.VMEM((a.shape[0], width), jnp.float32),
                 pltpu.SemaphoreType.DMA((4,)),
-                pltpu.SemaphoreType.DMA((2, 12)),
-                pltpu.SemaphoreType.DMA((16,)),
-                pltpu.SemaphoreType.DMA((16,)),
-                pltpu.SemaphoreType.DMA((2 * ncol, 3)),
-                pltpu.SemaphoreType.DMA((2, nz // 2, len(CHUNKS))),
-                pltpu.SemaphoreType.DMA((nz, len(CHUNKS))),
+                pltpu.SemaphoreType.DMA,
+                pltpu.SemaphoreType.DMA((D_FIRST + 8,)),
+                pltpu.SemaphoreType.DMA,
+                pltpu.SemaphoreType.DMA(((nz // 2 - 1) * len(CHUNKS) + 1,)),
             ],
             compiler_params=pltpu.CompilerParams(
-                collective_id=0, has_side_effects=True, vmem_limit_bytes=58 * 2**20
+                collective_id=0, has_side_effects=True, vmem_limit_bytes=46 * 2**20
             ),
-        )(a, am, b, bm)
+        )(*(pltpu.with_memory_space_constraint(v, pltpu.HBM) for v in (a, am, b, bm)))
 
     spec = P("row", "col")
     return jax.shard_map(

time: 38.8 us -> 34.8 us (0.90)
  Pallas kernels: 36.4 us -> 33.7 us
  local copies, waits for them, and re-layouts: 2.26 us -> 0.97 us
    pallas_call x1, Pallas kernels: 36.4 us -> 33.7 us  [per_device(): pl.pallas_call(functools.partial(kernel, nz, nx, rows), out_shape=jax.Sha...]
    unnamed x1, local copies, waits for them, and re-layouts: 2.26 us -> 0.97 us
where the time goes in v3:
time: 34.8 us; the launch traced here: 34.7 us
  Pallas kernels  33.7 us (97%)
  local copies, waits for them, and re-layouts  0.97 us (3%)
    pallas_call x1, Pallas kernels, per_device(): pl.pallas_call(functools.partial(kernel, nz, nx, rows), out_shape=jax.Sha...  33.7 us
    unnamed x1, local copies, waits for them, and re-layouts  0.97 us

profile of v3, /device:TPU:1, one launch (start us, length us, event | category | flops | bytes accessed | tf_op | source)
XLA Modules:
  0.0 34.7 jit_solution(8545902376862667321)
XLA Ops:
  0.0 33.7 %shard_map.46 = bf16[2048,256]{1,0:T(8,128)(2,1)S(1)} custom-call(bf16[2048,256]{1,0:T(8,128)(2,1)} %a_ref.1, s32[1,8]{1,0:T(1,128)} %bitcast.1, bf16[512,512]{1,0:T(8,128)(2,1)} %b_ref.1, s32[2,2]{1,0:T(2,128)} %bm_ref.1), custom_call_target="tpu_custom_call" | custom-call | tf_op jit(solution)/shard_map/pallas_call | solution.py:280
  33.7 1.0 %copy.6 = bf16[2048,256]{1,0:T(8,128)(2,1)} copy(bf16[2048,256]{1,0:T(8,128)(2,1)S(1)} %shard_map.46) | data formatting | bytes 2097152

commit v4 on v3

--- a/solution.py
+++ b/solution.py
@@ -216,10 +216,25 @@
 
         lax.fori_loop(0, BS // TILE, body, 0)
 
-    def multiply(source, first=False):
-        total = jnp.dot(dense[source], bbuf[source], preferred_element_type=jnp.float32)
-        acc[...] = total if first else acc[...] + total
-
+    def multiply(panels, hops, panels_before=0, hops_before=0):
+        def body(i, _):
+            source = (z + nz + i - hops) % nz
+            n = (source // 2 + nx - x) % nx
+            near = jnp.where(source % 2 == yl, 1, 0)
+            place = jnp.where(n == 0, 1 - near, jnp.where(n == nx - 1, 0, n) + 5 - 3 * near)
+            far_off = jnp.abs(i - hops)
+            ready = place < panels
+            done = (far_off <= hops_before) & (place < panels_before)
+
+            @pl.when(ready & jnp.logical_not(done))
+            def _():
+                acc[...] += jnp.dot(dense[source], bbuf[source], preferred_element_type=jnp.float32)
+
+            return 0
+
+        lax.fori_loop(0, 2 * hops + 1, body, 0)
+
+    acc[...] = jnp.zeros_like(acc)
     expand(0, 0)
     b_step(1, 0)
     x_arrival(0)
@@ -232,6 +247,7 @@
     b_step(1, 3)
     y_arrival(0)
     x_arrival(3)
+    multiply(2, 1, 0, 0)
     b_step(2, 0)
     y_arrival(1)
     x_second(1)
@@ -240,25 +256,22 @@
     y_arrival(2)
     x_second(2)
     expand(2, 0)
+    multiply(4, 1, 2, 1)
     b_step(2, 2)
     y_arrival(3)
+    b_step(2, 3)
+    y_far()
     expand(3, 0)
-    b_step(2, 3)
     expand(1, 1)
-    y_far()
+    b_step(3, 0)
     expand(2, 1)
-    b_step(3, 0)
+    multiply(7, 2, 4, 1)
     expand(3, 1)
     b_step(3, 1)
-    multiply(z, True)
     b_step(3, 2)
-    multiply((z + 1) % nz)
+    multiply(8, 2, 7, 2)
     b_step(3, 3)
-    multiply((z + nz - 1) % nz)
-    multiply((z + 2) % nz)
-    multiply((z + nz - 2) % nz)
-    multiply((z + 3) % nz)
-    multiply((z + nz - 3) % nz)
+    multiply(8, 3, 8, 2)
     b_wait(b_recv.at[(far - 1) * len(CHUNKS)], b_ref.shape[0])
     last = (z + far) % nz
     total = jnp.dot(dense[last], bbuf[last], preferred_element_type=jnp.float32)

time: 34.8 us -> 32.9 us (0.945)
  Pallas kernels: 33.7 us -> 31.8 us
    pallas_call x1, Pallas kernels: 33.7 us -> 31.8 us  [per_device(): pl.pallas_call(functools.partial(kernel, nz, nx, rows), out_shape=jax.Sha...]
where the time goes in v4:
time: 32.9 us; the launch traced here: 32.8 us
  Pallas kernels  31.8 us (97%)
  local copies, waits for them, and re-layouts  0.97 us (3%)
    pallas_call x1, Pallas kernels, per_device(): pl.pallas_call(functools.partial(kernel, nz, nx, rows), out_shape=jax.Sha...  31.8 us
    unnamed x1, local copies, waits for them, and re-layouts  0.97 us

profile of v4, /device:TPU:1, one launch (start us, length us, event | category | flops | bytes accessed | tf_op | source)
XLA Modules:
  0.0 32.8 jit_solution(14392731805467993295)
XLA Ops:
  0.0 31.8 %shard_map.46 = bf16[2048,256]{1,0:T(8,128)(2,1)S(1)} custom-call(bf16[2048,256]{1,0:T(8,128)(2,1)} %a_ref.1, s32[1,8]{1,0:T(1,128)} %bitcast.1, bf16[512,512]{1,0:T(8,128)(2,1)} %b_ref.1, s32[2,2]{1,0:T(2,128)} %bm_ref.1), custom_call_target="tpu_custom_call" | custom-call | tf_op jit(solution)/shard_map/pallas_call | solution.py:293
  31.8 1.0 %copy.6 = bf16[2048,256]{1,0:T(8,128)(2,1)} copy(bf16[2048,256]{1,0:T(8,128)(2,1)S(1)} %shard_map.46) | data formatting | bytes 2097152

commit v5 on v4

--- a/solution.py
+++ b/solution.py
@@ -68,18 +68,32 @@
             device_id_type=MESH,
         )
 
+    first = jnp.where((z + nz // 4) % nz < nz // 2, 1, 0)
+    second = 1 - first
+
     def b_send_to(source, j, way, hop):
-        sem = b_recv.at[(hop - 1) * len(CHUNKS) + j if hop < far else (far - 1) * len(CHUNKS)]
-        remote(bbuf.at[source, pl.ds(*CHUNKS[j])], b_send, sem, dev_z[way]).start()
+        sem = b_recv.at[way, (hop - 1) * len(CHUNKS) + j] if hop < far else b_recv.at[0, (far - 1) * len(CHUNKS)]
+        dev = {"row": (z + nz + 1 - 2 * way) % nz}
+        remote(bbuf.at[source, pl.ds(*CHUNKS[j])], b_send, sem, dev).start()
 
     def b_wait(sem, lines):
         remote(bbuf.at[z, pl.ds(0, lines)], b_send, sem, dev_z[0]).wait_recv()
 
+    def b_half(way, hop, j):
+        b_wait(b_recv.at[way, (hop - 1) * len(CHUNKS) + j], CHUNKS[j][1])
+        onward = functools.partial(b_send_to, (z + nz + (2 * way - 1) * hop) % nz, j, way, hop + 1)
+        if hop + 1 < far:
+            onward()
+        else:
+            to = (z + nz + 1 - 2 * way) % nz
+            takes = WAYS[j]
+            takes = jnp.where(((to == 0)), 1, takes)
+            takes = jnp.where(((to == 3)), 0, takes)
+            pl.when(way == takes)(onward)
+
     def b_step(hop, j):
-        b_wait(b_recv.at[(hop - 1) * len(CHUNKS) + j], 2 * CHUNKS[j][1])
-        for way in range(2):
-            if hop + 1 < far or WAYS[j] == way:
-                b_send_to(((z + nz - hop) % nz, (z + hop) % nz)[way], j, way, hop + 1)
+        b_half(first, hop, j)
+        b_half(second, hop, j)
 
     def a_send_to(item, slot, part, sem, dev):
         start, size = ((0, BS + CODE), (0, HALF), (HALF, HALF + CODE))[part]
@@ -236,47 +250,63 @@
 
     acc[...] = jnp.zeros_like(acc)
     expand(0, 0)
-    b_step(1, 0)
+    b_half(first, 1, 0)
+    b_half(first, 1, 1)
+    b_half(second, 1, 0)
     x_arrival(0)
-    b_step(1, 1)
+    b_half(first, 1, 2)
+    b_half(second, 1, 1)
     x_arrival(1)
     y_own()
-    b_step(1, 2)
+    b_half(first, 1, 3)
+    b_half(second, 1, 2)
     x_arrival(2)
     expand(0, 1)
-    b_step(1, 3)
+    b_half(first, 2, 0)
+    b_half(second, 1, 3)
     y_arrival(0)
     x_arrival(3)
     multiply(2, 1, 0, 0)
-    b_step(2, 0)
+    b_half(first, 2, 1)
+    b_half(second, 2, 0)
     y_arrival(1)
     x_second(1)
     expand(1, 0)
-    b_step(2, 1)
+    b_half(first, 2, 2)
+    b_half(second, 2, 1)
     y_arrival(2)
     x_second(2)
     expand(2, 0)
     multiply(4, 1, 2, 1)
-    b_step(2, 2)
+    b_half(first, 2, 3)
+    b_half(second, 2, 2)
     y_arrival(3)
-    b_step(2, 3)
+    b_half(first, 3, 0)
+    b_half(second, 2, 3)
     y_far()
     expand(3, 0)
     expand(1, 1)
-    b_step(3, 0)
+    b_half(first, 3, 1)
+    b_half(second, 3, 0)
     expand(2, 1)
     multiply(7, 2, 4, 1)
     expand(3, 1)
-    b_step(3, 1)
-    b_step(3, 2)
+    b_half(first, 3, 2)
+    b_half(second, 3, 1)
+    b_half(first, 3, 3)
+    b_half(second, 3, 2)
     multiply(8, 2, 7, 2)
-    b_step(3, 3)
+    b_half(second, 3, 3)
     multiply(8, 3, 8, 2)
-    b_wait(b_recv.at[(far - 1) * len(CHUNKS)], b_ref.shape[0])
+    b_wait(b_recv.at[0, (far - 1) * len(CHUNKS)], b_ref.shape[0])
     last = (z + far) % nz
     total = jnp.dot(dense[last], bbuf[last], preferred_element_type=jnp.float32)
     c_ref[...] = (acc[...] + total).astype(jnp.bfloat16)
-    remote(bbuf.at[pl.ds(0, nz - 1)], b_send, b_recv.at[0], dev_z[0]).wait_send()
+    remote(bbuf.at[pl.ds(0, nz - 2)], b_send, b_recv.at[0, 0], dev_z[0]).wait_send()
+    pl.when(((z == 4) | (z == 7)))(remote(bbuf.at[0, pl.ds(0, BS)], b_send, b_recv.at[0, 0], dev_z[0]).wait_send)
+    pl.when(((z == 0) | (z == 3) | (z == 5) | (z == 6)))(remote(bbuf.at[pl.ds(0, 1)], b_send, b_recv.at[0, 0], dev_z[0]).wait_send)
+    pl.when(((z == 1) | (z == 2)))(remote(abuf.at[0, pl.ds(0, BS)], b_send, b_recv.at[0, 0], dev_z[0]).wait_send)
+    pl.when(((z == 1) | (z == 2)))(remote(bbuf.at[pl.ds(0, 1)], b_send, b_recv.at[0, 0], dev_z[0]).wait_send)
     remote(abuf.at[pl.ds(0, 30)], a_send, a_recv.at[0], dev_d).wait_send()
 
 
@@ -308,7 +338,7 @@
                 pltpu.SemaphoreType.DMA,
                 pltpu.SemaphoreType.DMA((D_FIRST + 8,)),
                 pltpu.SemaphoreType.DMA,
-                pltpu.SemaphoreType.DMA(((nz // 2 - 1) * len(CHUNKS) + 1,)),
+                pltpu.SemaphoreType.DMA((2, (nz // 2 - 1) * len(CHUNKS) + 1)),
             ],
             compiler_params=pltpu.CompilerParams(
                 collective_id=0, has_side_effects=True, vmem_limit_bytes=46 * 2**20

time: 32.9 us -> 32.1 us (0.976)
  Pallas kernels: 31.8 us -> 31 us
    pallas_call x1, Pallas kernels: 31.8 us -> 31 us  [per_device(): pl.pallas_call(functools.partial(kernel, nz, nx, rows), out_shape=jax.Sha...]
where the time goes in v5:
time: 32.1 us; the launch traced here: 32 us
  Pallas kernels  31 us (97%)
  local copies, waits for them, and re-layouts  0.97 us (3%)
    pallas_call x1, Pallas kernels, per_device(): pl.pallas_call(functools.partial(kernel, nz, nx, rows), out_shape=jax.Sha...  31 us
    unnamed x1, local copies, waits for them, and re-layouts  0.97 us

profile of v5, /device:TPU:1, one launch (start us, length us, event | category | flops | bytes accessed | tf_op | source)
XLA Modules:
  0.0 32.0 jit_solution(6027398902315767060)
XLA Ops:
  0.0 31.0 %shard_map.46 = bf16[2048,256]{1,0:T(8,128)(2,1)S(1)} custom-call(bf16[2048,256]{1,0:T(8,128)(2,1)} %a_ref.1, s32[1,8]{1,0:T(1,128)} %bitcast.1, bf16[512,512]{1,0:T(8,128)(2,1)} %b_ref.1, s32[2,2]{1,0:T(2,128)} %bm_ref.1), custom_call_target="tpu_custom_call" | custom-call | tf_op jit(solution)/shard_map/pallas_call | solution.py:323
  31.0 1.0 %copy.6 = bf16[2048,256]{1,0:T(8,128)(2,1)} copy(bf16[2048,256]{1,0:T(8,128)(2,1)S(1)} %shard_map.46) | data formatting | bytes 2097152

commit v6 on v5

--- a/solution.py
+++ b/solution.py
@@ -111,6 +111,7 @@
     def a_wait(sem, part):
         b_wait(a_recv.at[sem], 2 * (0, HALF, HALF + CODE)[part])
 
+    acc[...] = jnp.zeros_like(acc)
     load_bm.wait()
     load_b.wait()
     for start, size in CHUNKS:
@@ -248,7 +249,6 @@
 
         lax.fori_loop(0, 2 * hops + 1, body, 0)
 
-    acc[...] = jnp.zeros_like(acc)
     expand(0, 0)
     b_half(first, 1, 0)
     b_half(first, 1, 1)
@@ -281,15 +281,16 @@
     b_half(first, 2, 3)
     b_half(second, 2, 2)
     y_arrival(3)
+    expand(3, 0)
     b_half(first, 3, 0)
     b_half(second, 2, 3)
+    multiply(5, 2, 4, 1)
     y_far()
-    expand(3, 0)
     expand(1, 1)
     b_half(first, 3, 1)
     b_half(second, 3, 0)
     expand(2, 1)
-    multiply(7, 2, 4, 1)
+    multiply(7, 2, 5, 2)
     expand(3, 1)
     b_half(first, 3, 2)
     b_half(second, 3, 1)

time: 32.1 us -> 31.5 us (0.981)
  Pallas kernels: 31 us -> 30.1 us
    pallas_call x1, Pallas kernels: 31 us -> 30.1 us  [per_device(): pl.pallas_call(functools.partial(kernel, nz, nx, rows), out_shape=jax.Sha...]
where the time goes in v6:
time: 31.5 us; the launch traced here: 31.1 us
  Pallas kernels  30.1 us (96%)
  local copies, waits for them, and re-layouts  0.97 us (3%)
    pallas_call x1, Pallas kernels, per_device(): pl.pallas_call(functools.partial(kernel, nz, nx, rows), out_shape=jax.Sha...  30.1 us
    unnamed x1, local copies, waits for them, and re-layouts  0.97 us

profile of v6, /device:TPU:1, one launch (start us, length us, event | category | flops | bytes accessed | tf_op | source)
XLA Modules:
  0.0 31.1 jit_solution(3991120587166796192)
XLA Ops:
  0.0 30.1 %shard_map.46 = bf16[2048,256]{1,0:T(8,128)(2,1)S(1)} custom-call(bf16[2048,256]{1,0:T(8,128)(2,1)} %a_ref.1, s32[1,8]{1,0:T(1,128)} %bitcast.1, bf16[512,512]{1,0:T(8,128)(2,1)} %b_ref.1, s32[2,2]{1,0:T(2,128)} %bm_ref.1), custom_call_target="tpu_custom_call" | custom-call | tf_op jit(solution)/shard_map/pallas_call | solution.py:324
  30.1 1.0 %copy.6 = bf16[2048,256]{1,0:T(8,128)(2,1)} copy(bf16[2048,256]{1,0:T(8,128)(2,1)S(1)} %shard_map.46) | data formatting | bytes 2097152

commit v7 on v6

--- a/solution.py
+++ b/solution.py
@@ -284,13 +284,13 @@
     expand(3, 0)
     b_half(first, 3, 0)
     b_half(second, 2, 3)
-    multiply(5, 2, 4, 1)
+    expand(1, 1)
+    multiply(6, 2, 4, 1)
     y_far()
-    expand(1, 1)
     b_half(first, 3, 1)
     b_half(second, 3, 0)
     expand(2, 1)
-    multiply(7, 2, 5, 2)
+    multiply(7, 2, 6, 2)
     expand(3, 1)
     b_half(first, 3, 2)
     b_half(second, 3, 1)

time: 31.5 us -> 32.4 us (1.029)
  Pallas kernels: 30.1 us -> 31.2 us
    pallas_call x1, Pallas kernels: 30.1 us -> 31.2 us  [per_device(): pl.pallas_call(functools.partial(kernel, nz, nx, rows), out_shape=jax.Sha...]
where the time goes in v7:
time: 32.4 us; the launch traced here: 32.2 us
  Pallas kernels  31.2 us (96%)
  local copies, waits for them, and re-layouts  0.97 us (3%)
    pallas_call x1, Pallas kernels, per_device(): pl.pallas_call(functools.partial(kernel, nz, nx, rows), out_shape=jax.Sha...  31.2 us
    unnamed x1, local copies, waits for them, and re-layouts  0.97 us

profile of v7, /device:TPU:1, one launch (start us, length us, event | category | flops | bytes accessed | tf_op | source)
XLA Modules:
  0.0 32.2 jit_solution(16139568513332166476)
XLA Ops:
  0.0 31.2 %shard_map.46 = bf16[2048,256]{1,0:T(8,128)(2,1)S(1)} custom-call(bf16[2048,256]{1,0:T(8,128)(2,1)} %a_ref.1, s32[1,8]{1,0:T(1,128)} %bitcast.1, bf16[512,512]{1,0:T(8,128)(2,1)} %b_ref.1, s32[2,2]{1,0:T(2,128)} %bm_ref.1), custom_call_target="tpu_custom_call" | custom-call | tf_op jit(solution)/shard_map/pallas_call | solution.py:324
  31.2 1.0 %copy.6 = bf16[2048,256]{1,0:T(8,128)(2,1)} copy(bf16[2048,256]{1,0:T(8,128)(2,1)S(1)} %shard_map.46) | data formatting | bytes 2097152
